TPU v7x, 32 devices: a whole 2x2x4 slice. The times are simulated.
32 devices in a mesh: dp: 4 (over z), fsdp: 8 (over y, x, core).
Axes of the slice: x: 2, y: 2, z: 4, core: 2. Of those that a mesh axis runs over, the one named last changes fastest.
Arguments:
- tokens: bfloat16 [32768, 768], P(('dp', 'fsdp')), may hold values from -6 to 6
- block_bucket: int32 [512], P(('dp', 'fsdp')), may hold values from 64 to 512, as said below
- lengths: int32 [512], P(('dp', 'fsdp')), may hold values from 0 to 512, as said below
- query_weight: bfloat16 [768, 768], P(('dp', 'fsdp')), may hold values from -0.3125 to 0.3125
- query_bias: bfloat16 [768], P(('dp', 'fsdp')), may hold values from -1 to 1
- key_weight: bfloat16 [768, 768], P(('dp', 'fsdp')), may hold values from -0.3125 to 0.3125
- value_weight: bfloat16 [768, 768], P(('dp', 'fsdp')), may hold values from -0.21875 to 0.21875
- value_bias: bfloat16 [768], P(('dp', 'fsdp')), may hold values from -1 to 1
- out_weight: bfloat16 [768, 768], P(('dp', 'fsdp')), may hold values from -0.875 to 0.875
- out_bias: bfloat16 [768], P(('dp', 'fsdp')), may hold values from -1 to 1
- first_gain: bfloat16 [768], P(('dp', 'fsdp')), may hold values from 0.5 to 1.5
- first_shift: bfloat16 [768], P(('dp', 'fsdp')), may hold values from -1 to 1
- up_weight: bfloat16 [768, 3072], P(('dp', 'fsdp')), may hold values from -0.21875 to 0.21875
- up_bias: bfloat16 [3072], P(('dp', 'fsdp')), may hold values from -1 to 1
- down_weight: bfloat16 [3072, 768], P(('dp', 'fsdp')), may hold values from -0.109375 to 0.109375
- down_bias: bfloat16 [768], P(('dp', 'fsdp')), may hold values from -1 to 1
- second_gain: bfloat16 [768], P(('dp', 'fsdp')), may hold values from 0.5 to 1.5
- second_shift: bfloat16 [768], P(('dp', 'fsdp')), may hold values from -1 to 1
- out_grad: bfloat16 [32768, 768], P(('dp', 'fsdp')), may hold values from -6 to 6
- pool_grad: float32 [512, 1728], P(('dp', 'fsdp')), may hold values from -6 to 6
Outputs:
- layer_out: bfloat16 [32768, 768], P(('dp', 'fsdp'))
- pools: float32 [512, 1728], P(('dp', 'fsdp'))
- token_grad: float32 [32768, 768], P(('dp', 'fsdp'))
- grad_query_weight: float32 [768, 768], P(('dp', 'fsdp'))
- grad_query_bias: float32 [768], P(('dp', 'fsdp'))
- grad_key_weight: float32 [768, 768], P(('dp', 'fsdp'))
- grad_value_weight: float32 [768, 768], P(('dp', 'fsdp'))
- grad_value_bias: float32 [768], P(('dp', 'fsdp'))
- grad_out_weight: float32 [768, 768], P(('dp', 'fsdp'))
- grad_out_bias: float32 [768], P(('dp', 'fsdp'))
- grad_first_gain: float32 [768], P(('dp', 'fsdp'))
- grad_first_shift: float32 [768], P(('dp', 'fsdp'))
- grad_up_weight: float32 [768, 3072], P(('dp', 'fsdp'))
- grad_up_bias: float32 [3072], P(('dp', 'fsdp'))
- grad_down_weight: float32 [3072, 768], P(('dp', 'fsdp'))
- grad_down_bias: float32 [768], P(('dp', 'fsdp'))
- grad_second_gain: float32 [768], P(('dp', 'fsdp'))
- grad_second_shift: float32 [768], P(('dp', 'fsdp'))
Inputs may be any that keep to these rules, and one draw needn't show every extreme that they name: `block_bucket`: each row of 512 tokens is cut into buckets of 64 times a power of two tokens, each aligned to its size; every block gives the size of its bucket. `lengths`: at the first block of a bucket the length of its sentence, from 8 to the bucket's size and over half of it in buckets larger than 64; 0 at the other blocks; the first sentence has 512 tokens.
All inputs are finite; a program needn't handle non-finite values.
Results may differ from a plain program's by a relative error of at most 0.014.
The roundings to bfloat16 on the way count: a program that leaves them out, or rounds other values in their place, can miss the bound.
Values may be sent and summed in bfloat16 or wider, within the bound.
A program may use at most 192 MiB of HBM per device.

v0:
```python
import jax
import jax.numpy as jnp
from jax import lax
from jax.sharding import PartitionSpec as P

D = 768
HEADS = 12
HD = 64
ROW = 512
BLOCK = 64


def dense(left, right):
    return jnp.dot(left, right, preferred_element_type=jnp.float32)


def product(left, right):
    return jnp.dot(left, right, precision=lax.Precision.HIGHEST, preferred_element_type=jnp.float32)


def layer_norm(values, scales, offset):
    center = values - jnp.mean(values, axis=-1, keepdims=True)
    spread = jnp.mean(center * center, axis=-1, keepdims=True)
    return center * lax.rsqrt(spread + 1e-05) * scales + offset


def pool_breadths(model_width):
    return [
        model_width,
        2 * model_width // 3,
        model_width // 3,
        model_width // 6,
        model_width // 12,
    ]


def matryoshka(averages, model_width):
    pieces = []
    for breadth in pool_breadths(model_width):
        leading = averages[:, :breadth]
        pieces.append(
            leading * lax.rsqrt(jnp.mean(leading * leading, axis=-1, keepdims=True) + 1e-06)
        )
    return jnp.concatenate(pieces, axis=-1)


def gelu_exact(values):
    return jax.nn.gelu(values, approximate=False)


def sentence_layout(block_bucket, lengths, block_size):
    block_count = block_bucket.shape[0]
    blocks = jnp.arange(block_count, dtype=jnp.int32)
    stride = block_bucket // block_size
    start_block = blocks // stride * stride
    block_len = jnp.sum(
        jnp.where(start_block[:, None] == blocks[None, :], lengths[None, :], 0), axis=1
    )
    token_start = jnp.repeat(start_block * block_size, block_size)
    token_len = jnp.repeat(block_len, block_size)
    positions = jnp.arange(block_count * block_size, dtype=jnp.int32)
    valid = positions - token_start < token_len
    member = (token_start[None, :] == (start_block * block_size)[:, None]) & valid[None, :]
    pool_matrix = (
        jnp.where(member, 1.0, 0.0).astype(jnp.float32) / block_len.astype(jnp.float32)[:, None]
    )
    return (token_start, valid, pool_matrix)


def masked_scores(query_rows, key_rows, start_rows, valid_rows):
    allowed = (start_rows[:, None] == start_rows[None, :]) & valid_rows[None, :]
    scores = (
        jnp.einsum("qhd,khd->hqk", query_rows, key_rows, preferred_element_type=jnp.float32) * 0.125
    )
    return jnp.where(allowed[None], scores, -1e30)


def attend_forward(items):
    query_rows, key_rows, value_rows, start_rows, valid_rows = items
    scores = masked_scores(query_rows, key_rows, start_rows, valid_rows)
    row_peak = jnp.max(scores, axis=-1, keepdims=True)
    exponent = jnp.exp(scores - row_peak)
    row_total = jnp.sum(exponent, axis=-1, keepdims=True)
    softmax_out = (exponent / row_total).astype(jnp.bfloat16)
    context = jnp.einsum(
        "hqk,khd->qhd", softmax_out, value_rows, preferred_element_type=jnp.float32
    )
    return (context.astype(jnp.bfloat16), row_peak + jnp.log(row_total))


def attend_backward(items):
    query_rows, key_rows, value_rows, grad_rows, log_total, start_rows, valid_rows = items
    scores = masked_scores(query_rows, key_rows, start_rows, valid_rows)
    softmax_out = jnp.exp(scores - log_total)
    grad_value_rows = jnp.einsum(
        "hqk,qhd->khd",
        softmax_out.astype(jnp.bfloat16),
        grad_rows,
        preferred_element_type=jnp.float32,
    )
    grad_probs = jnp.einsum(
        "qhd,khd->hqk", grad_rows, value_rows, preferred_element_type=jnp.float32
    )
    row_delta = jnp.sum(softmax_out * grad_probs, axis=-1, keepdims=True)
    grad_scores = (softmax_out * (grad_probs - row_delta)).astype(jnp.bfloat16)
    grad_query_rows = (
        jnp.einsum("hqk,khd->qhd", grad_scores, key_rows, preferred_element_type=jnp.float32)
        * 0.125
    )
    grad_key_rows = (
        jnp.einsum("hqk,qhd->khd", grad_scores, query_rows, preferred_element_type=jnp.float32)
        * 0.125
    )
    return (
        grad_query_rows.astype(jnp.bfloat16),
        grad_key_rows.astype(jnp.bfloat16),
        grad_value_rows.astype(jnp.bfloat16),
    )


def body(
    tokens,
    block_bucket,
    lengths,
    query_weight,
    query_bias,
    key_weight,
    value_weight,
    value_bias,
    out_weight,
    out_bias,
    first_gain,
    first_shift,
    up_weight,
    up_bias,
    down_weight,
    down_bias,
    second_gain,
    second_shift,
    out_grad,
    pool_grad,
):
    attn_full = (
        lax.all_gather(query_weight, ("dp", "fsdp"), axis=0, tiled=True),
        lax.all_gather(key_weight, ("dp", "fsdp"), axis=0, tiled=True),
        lax.all_gather(value_weight, ("dp", "fsdp"), axis=0, tiled=True),
        lax.all_gather(out_weight, ("dp", "fsdp"), axis=0, tiled=True),
        lax.all_gather(query_bias, ("dp", "fsdp"), axis=0, tiled=True),
        lax.all_gather(value_bias, ("dp", "fsdp"), axis=0, tiled=True),
        lax.all_gather(out_bias, ("dp", "fsdp"), axis=0, tiled=True),
        lax.all_gather(first_gain, ("dp", "fsdp"), axis=0, tiled=True),
        lax.all_gather(first_shift, ("dp", "fsdp"), axis=0, tiled=True),
    )
    ffn_full = (
        lax.all_gather(up_weight, ("dp", "fsdp"), axis=0, tiled=True),
        lax.all_gather(down_weight, ("dp", "fsdp"), axis=0, tiled=True),
        lax.all_gather(up_bias, ("dp", "fsdp"), axis=0, tiled=True),
        lax.all_gather(down_bias, ("dp", "fsdp"), axis=0, tiled=True),
        lax.all_gather(second_gain, ("dp", "fsdp"), axis=0, tiled=True),
        lax.all_gather(second_shift, ("dp", "fsdp"), axis=0, tiled=True),
    )
    full_query, full_key, full_value, full_out = (
        attn_full[0],
        attn_full[1],
        attn_full[2],
        attn_full[3],
    )
    bias_query = attn_full[4].astype(jnp.float32)
    bias_value = attn_full[5].astype(jnp.float32)
    bias_out = attn_full[6].astype(jnp.float32)
    gain_first = attn_full[7].astype(jnp.float32)
    shift_first = attn_full[8].astype(jnp.float32)
    full_up, full_down = (ffn_full[0], ffn_full[1])
    bias_up = ffn_full[2].astype(jnp.float32)
    bias_down = ffn_full[3].astype(jnp.float32)
    gain_second = ffn_full[4].astype(jnp.float32)
    shift_second = ffn_full[5].astype(jnp.float32)
    token_start, valid, pool_matrix = sentence_layout(block_bucket, lengths, BLOCK)
    row_count = tokens.shape[0] // ROW

    def by_rows(array):
        return array.reshape((row_count, ROW) + array.shape[1:])

    def split_heads(array):
        return array.reshape(row_count, ROW, HEADS, HD)

    queries = (dense(tokens, full_query) + bias_query).astype(jnp.bfloat16)
    keys_all = dense(tokens, full_key).astype(jnp.bfloat16)
    values_all = (dense(tokens, full_value) + bias_value).astype(jnp.bfloat16)
    context, log_total = lax.map(
        attend_forward,
        (
            split_heads(queries),
            split_heads(keys_all),
            split_heads(values_all),
            by_rows(token_start),
            by_rows(valid),
        ),
    )
    context_low = context.reshape(-1, D)
    first_sum = tokens.astype(jnp.float32) + dense(context_low, full_out) + bias_out
    hidden_f, first_back = jax.vjp(layer_norm, first_sum, gain_first, shift_first)
    hidden_low = hidden_f.astype(jnp.bfloat16)
    pre_gelu = dense(hidden_low, full_up) + bias_up
    activated = gelu_exact(pre_gelu).astype(jnp.bfloat16)
    second_sum = hidden_low.astype(jnp.float32) + dense(activated, full_down) + bias_down
    outputs, second_back = jax.vjp(layer_norm, second_sum, gain_second, shift_second)
    pools, pool_back = jax.vjp(
        lambda rows_in: matryoshka(product(pool_matrix, rows_in), D), outputs
    )
    ffn_back = (
        lax.all_gather(up_weight, ("dp", "fsdp"), axis=0, tiled=True),
        lax.all_gather(down_weight, ("dp", "fsdp"), axis=0, tiled=True),
        lax.all_gather(up_bias, ("dp", "fsdp"), axis=0, tiled=True),
        lax.all_gather(down_bias, ("dp", "fsdp"), axis=0, tiled=True),
        lax.all_gather(second_gain, ("dp", "fsdp"), axis=0, tiled=True),
        lax.all_gather(second_shift, ("dp", "fsdp"), axis=0, tiled=True),
    )
    up_back, down_back = (ffn_back[0], ffn_back[1])
    out_total = out_grad.astype(jnp.float32) + pool_back(pool_grad)[0]
    grad_second_sum, grad_gain_second, grad_shift_second = second_back(out_total)
    grad_branch = grad_second_sum.astype(jnp.bfloat16)
    grad_bias_down = jnp.sum(grad_branch.astype(jnp.float32), axis=0)
    grad_down = jnp.einsum("tf,td->fd", activated, grad_branch, preferred_element_type=jnp.float32)
    grad_activated = jnp.einsum(
        "td,fd->tf", grad_branch, down_back, preferred_element_type=jnp.float32
    )
    grad_pre = jax.vjp(gelu_exact, pre_gelu)[1](grad_activated)[0].astype(jnp.bfloat16)
    grad_bias_up = jnp.sum(grad_pre.astype(jnp.float32), axis=0)
    grad_up = jnp.einsum("td,tf->df", hidden_low, grad_pre, preferred_element_type=jnp.float32)
    grad_hidden = grad_second_sum + jnp.einsum(
        "tf,df->td", grad_pre, up_back, preferred_element_type=jnp.float32
    )
    ffn_grads = (
        lax.psum_scatter(grad_up, ("dp", "fsdp"), scatter_dimension=0, tiled=True),
        lax.psum_scatter(grad_down, ("dp", "fsdp"), scatter_dimension=0, tiled=True),
        lax.psum_scatter(grad_bias_up, ("dp", "fsdp"), scatter_dimension=0, tiled=True),
        lax.psum_scatter(grad_bias_down, ("dp", "fsdp"), scatter_dimension=0, tiled=True),
        lax.psum_scatter(grad_gain_second, ("dp", "fsdp"), scatter_dimension=0, tiled=True),
        lax.psum_scatter(grad_shift_second, ("dp", "fsdp"), scatter_dimension=0, tiled=True),
    )
    attn_back = (
        lax.all_gather(query_weight, ("dp", "fsdp"), axis=0, tiled=True),
        lax.all_gather(key_weight, ("dp", "fsdp"), axis=0, tiled=True),
        lax.all_gather(value_weight, ("dp", "fsdp"), axis=0, tiled=True),
        lax.all_gather(out_weight, ("dp", "fsdp"), axis=0, tiled=True),
        lax.all_gather(query_bias, ("dp", "fsdp"), axis=0, tiled=True),
        lax.all_gather(value_bias, ("dp", "fsdp"), axis=0, tiled=True),
        lax.all_gather(out_bias, ("dp", "fsdp"), axis=0, tiled=True),
        lax.all_gather(first_gain, ("dp", "fsdp"), axis=0, tiled=True),
        lax.all_gather(first_shift, ("dp", "fsdp"), axis=0, tiled=True),
    )
    query_back, key_back, value_back, out_back = (
        attn_back[0],
        attn_back[1],
        attn_back[2],
        attn_back[3],
    )
    grad_first_sum, grad_gain_first, grad_shift_first = first_back(grad_hidden)
    grad_attended = grad_first_sum.astype(jnp.bfloat16)
    grad_bias_out = jnp.sum(grad_attended.astype(jnp.float32), axis=0)
    grad_out = jnp.einsum(
        "td,te->de", context_low, grad_attended, preferred_element_type=jnp.float32
    )
    grad_context = jnp.einsum(
        "te,de->td", grad_attended, out_back, preferred_element_type=jnp.float32
    ).astype(jnp.bfloat16)
    grad_queries, grad_keys, grad_values = lax.map(
        attend_backward,
        (
            split_heads(queries),
            split_heads(keys_all),
            split_heads(values_all),
            split_heads(grad_context),
            log_total,
            by_rows(token_start),
            by_rows(valid),
        ),
    )
    grad_queries = grad_queries.reshape(-1, D)
    grad_keys = grad_keys.reshape(-1, D)
    grad_values = grad_values.reshape(-1, D)
    grad_query = jnp.einsum("td,te->de", tokens, grad_queries, preferred_element_type=jnp.float32)
    grad_key = jnp.einsum("td,te->de", tokens, grad_keys, preferred_element_type=jnp.float32)
    grad_value = jnp.einsum("td,te->de", tokens, grad_values, preferred_element_type=jnp.float32)
    grad_bias_query = jnp.sum(grad_queries.astype(jnp.float32), axis=0)
    grad_bias_value = jnp.sum(grad_values.astype(jnp.float32), axis=0)
    token_grad = grad_first_sum + jnp.einsum(
        "te,de->td", grad_queries, query_back, preferred_element_type=jnp.float32
    )
    token_grad = token_grad + jnp.einsum(
        "te,de->td", grad_keys, key_back, preferred_element_type=jnp.float32
    )
    token_grad = token_grad + jnp.einsum(
        "te,de->td", grad_values, value_back, preferred_element_type=jnp.float32
    )
    attn_grads = (
        lax.psum_scatter(grad_query, ("dp", "fsdp"), scatter_dimension=0, tiled=True),
        lax.psum_scatter(grad_key, ("dp", "fsdp"), scatter_dimension=0, tiled=True),
        lax.psum_scatter(grad_value, ("dp", "fsdp"), scatter_dimension=0, tiled=True),
        lax.psum_scatter(grad_out, ("dp", "fsdp"), scatter_dimension=0, tiled=True),
        lax.psum_scatter(grad_bias_query, ("dp", "fsdp"), scatter_dimension=0, tiled=True),
        lax.psum_scatter(grad_bias_value, ("dp", "fsdp"), scatter_dimension=0, tiled=True),
        lax.psum_scatter(grad_bias_out, ("dp", "fsdp"), scatter_dimension=0, tiled=True),
        lax.psum_scatter(grad_gain_first, ("dp", "fsdp"), scatter_dimension=0, tiled=True),
        lax.psum_scatter(grad_shift_first, ("dp", "fsdp"), scatter_dimension=0, tiled=True),
    )
    return (
        outputs.astype(jnp.bfloat16),
        pools,
        token_grad,
        attn_grads[0],
        attn_grads[4],
        attn_grads[1],
        attn_grads[2],
        attn_grads[5],
        attn_grads[3],
        attn_grads[6],
        attn_grads[7],
        attn_grads[8],
        ffn_grads[0],
        ffn_grads[2],
        ffn_grads[1],
        ffn_grads[3],
        ffn_grads[4],
        ffn_grads[5],
    )


def solution(mesh):
    placed = (
        P(("dp", "fsdp"), None),
        P(("dp", "fsdp")),
        P(("dp", "fsdp")),
        P(("dp", "fsdp"), None),
        P(("dp", "fsdp")),
        P(("dp", "fsdp"), None),
        P(("dp", "fsdp"), None),
        P(("dp", "fsdp")),
        P(("dp", "fsdp"), None),
        P(("dp", "fsdp")),
        P(("dp", "fsdp")),
        P(("dp", "fsdp")),
        P(("dp", "fsdp"), None),
        P(("dp", "fsdp")),
        P(("dp", "fsdp"), None),
        P(("dp", "fsdp")),
        P(("dp", "fsdp")),
        P(("dp", "fsdp")),
        P(("dp", "fsdp"), None),
        P(("dp", "fsdp"), None),
    )
    return jax.shard_map(
        body,
        mesh=mesh,
        in_specs=placed,
        out_specs=(
            P(("dp", "fsdp"), None),
            P(("dp", "fsdp"), None),
            P(("dp", "fsdp"), None),
            P(("dp", "fsdp"), None),
            P(("dp", "fsdp")),
            P(("dp", "fsdp"), None),
            P(("dp", "fsdp"), None),
            P(("dp", "fsdp")),
            P(("dp", "fsdp"), None),
            P(("dp", "fsdp")),
            P(("dp", "fsdp")),
            P(("dp", "fsdp")),
            P(("dp", "fsdp"), None),
            P(("dp", "fsdp")),
            P(("dp", "fsdp"), None),
            P(("dp", "fsdp")),
            P(("dp", "fsdp")),
            P(("dp", "fsdp")),
        ),
        check_vma=False,
    )
```

profile of v0, /device:TPU:0, one launch (start us, length us, event | category | flops | bytes accessed | tf_op | source)
XLA Modules:
  0.0 1133.5 jit_solution(14906303134675754446)
XLA Ops:
  21.0 42.5 %all-reduce.23 = (bf16[768]{0:T(1024)(128)(2,1)S(1)}, bf16[768]{0:T(1024)(128)(2,1)S(1)}, bf16[768]{0:T(1024)(128)(2,1)S(1)}, bf16[768]{0:T(1024)(128)(2,1)S(1)}...) all-reduce(bf16[768]{0:T(1024)(128)(2,1)S(1)} %dynamic-update-slice, ...), channel_id=1, replica_groups=mesh['dp'=4,'fsdp'=8] {'dp','fsdp'}, use_global_device_ids=true, to_apply=%add.4 | all-reduce | flops 9216 | bytes 36864
  79.2 44.5 %all-gather.9.cloned.1.call-done = bf16[768,768]{1,0:T(8,128)(2,1)} async-done(((bf16[24,768]{1,0:T(8,128)(2,1)}), bf16[768,768]{1,0:T(8,128)(2,1)}) %all-gather.9.cloned.1.call-update) | async-done | bytes 1179664 | tf_op jit(solution)/shard_map/all_gather | solution.py:144
  128.7 50.9 %all-gather.11.cloned.1.call-done = bf16[768,768]{1,0:T(8,128)(2,1)} async-done(((bf16[24,768]{1,0:T(8,128)(2,1)}), bf16[768,768]{1,0:T(8,128)(2,1)}) %all-gather.11.cloned.1.call-update) | async-done | bytes 1179664 | tf_op jit(solution)/shard_map/all_gather | solution.py:145
  179.6 4.3 convolution_convert_fusion.1
  191.0 21.0 %while.26 = (s32[]{:T(128)}, bf16[2,512,12,64]{1,3,2,0:T(8,128)(2,1)}, f32[2,12,512,1]{2,1,3,0:T(8,128)S(1)}, bf16[2,512,12,64]{1,3,2,0:T(8,128)(2,1)}, s32[2,51...) while((s32[]{:T(128)}, ...), condition=%wide.region_4.5_spmd, body=%wide.region_1.4_spmd.sunk | while | flops 843966464 | bytes 42174056 | solution.py:190
  196.2 5.5 fusion.173
  206.6 5.5 fusion.173
  212.1 4.2 copy.134
  217.9 17.5 %all-gather.13.cloned.1.call-done = bf16[768,768]{1,0:T(8,128)(2,1)} async-done(((bf16[24,768]{1,0:T(8,128)(2,1)}), bf16[768,768]{1,0:T(8,128)(2,1)}) %all-gather.13.cloned.1.call-update) | async-done | bytes 1179664 | tf_op jit(solution)/shard_map/all_gather | solution.py:147
  235.4 3.8 fusion.111
  239.7 61.1 %all-gather.15.cloned.1.call-done = bf16[768,3072]{1,0:T(8,128)(2,1)} async-done(((bf16[24,3072]{1,0:T(8,128)(2,1)}), bf16[768,3072]{1,0:T(8,128)(2,1)}) %all-gather.15.cloned.1.call-update) | async-done | bytes 4718608 | tf_op jit(solution)/shard_map/all_gather | solution.py:155
  300.7 37.8 %multiply_convert_fusion.3 = (bf16[1024,3072]{1,0:T(8,128)(2,1)}, f32[1024,3072]{1,0:T(8,128)}, f32[1024,3072]{1,0:T(8,128)}) fusion(f32[3072]{0:T(1024)S(1)} %convert_element_type.134, bf16[768,3072]{1,0:T(8,128)(2,1)} %all-gather.15.cloned.1.call-done, f32[1024,768]{0,1:T(8,128)S(1)} %get-tuple-element.381, f32[768]{0:T(1024)S(1)} %convert_element_type.131, ...), kind=kOutput, calls=%fused_computation.70 | convolution fusion | flops 5043388416 | bytes 39348224 | tf_op jit(solution)/shard_map/dot_general | solution.py:14
  338.6 27.4 %all-gather.17.cloned.1.call-done = bf16[3072,768]{1,0:T(8,128)(2,1)} async-done(((bf16[96,768]{1,0:T(8,128)(2,1)}), bf16[3072,768]{1,0:T(8,128)(2,1)}) %all-gather.17.cloned.1.call-update) | async-done | bytes 4718608 | tf_op jit(solution)/shard_map/all_gather | solution.py:156
  366.0 9.3 fusion.112
  380.9 4.6 multiply_reduce_fusion.1
  390.1 19.1 %convert_reduce_fusion = (f32[3072]{0:T(1024)}, bf16[1024,3072]{1,0:T(8,128)(2,1)}) fusion(f32[1024,3072]{1,0:T(8,128)} %get-tuple-element.354, bf16[1024,768]{0,1:T(8,128)(2,1)} %get-tuple-element.346, bf16[3072,768]{1,0:T(8,128)(2,1)} %all-gather.17.cloned.1.call-done, f32[1024,3072]{1,0:T(8,128)} %get-tuple-element.382, f32[3072]{0:T(1024)S(1)} %convert_element_type.134), kind=kOutput, calls=%fused_computation.68 | convolution fusion | flops 4885312512 | bytes 37773312 | tf_op jit(solution)/shard_map/td,fd->tf/dot_general | solution.py:225
  409.2 10.3 multiply_reduce_fusion.2
  436.1 48.9 %while.27 = (s32[]{:T(128)}, bf16[2,512,12,64]{1,3,2,0:T(8,128)(2,1)}, bf16[2,512,12,64]{1,3,2,0:T(8,128)(2,1)}, bf16[2,512,12,64]{1,3,2,0:T(8,128)(2,1)}, bf16[...) while((s32[]{:T(128)}, ...), condition=%wide.region_25.26_spmd, body=%wide.region_23.25_spmd.sunk | while | flops 2062936064 | bytes 134943504 | solution.py:268
  438.7 6.9 multiply_reduce_fusion.18
  445.6 7.2 multiply_convert_fusion.5
  456.9 3.9 fusion.185
  463.0 6.9 multiply_reduce_fusion.18
  469.9 7.1 multiply_convert_fusion.5
  481.1 3.9 fusion.185
  514.6 10.6 fusion.113
  526.6 10.2 fusion.115
  539.1 40.7 %all-reduce.22 = (f32[768]{0:T(1024)S(1)}, f32[768]{0:T(1024)S(1)}, f32[768]{0:T(1024)S(1)}, f32[768]{0:T(1024)S(1)}, f32[768]{0:T(1024)S(1)}, /*index=5*/f32[30...) all-reduce(f32[768]{0:T(1024)S(1)} %reduce_sum.346, ...), channel_id=3, replica_groups=mesh['dp'=4,'fsdp'=8] {'dp','fsdp'}, use_global_device_ids=true, to_apply=%region_28.29.clone | all-reduce | flops 9216 | bytes 73728
  597.0 37.8 %reduce-scatter.19.cloned.1.call-done = f32[24,768]{1,0:T(8,128)} async-done(((f32[768,768]{1,0:T(8,128)}), f32[24,768]{1,0:T(8,128)}) %reduce-scatter.19.cloned.1.call-update) | async-done | bytes 73744
  634.8 103.9 %reduce-scatter.21.cloned.1.call-done = f32[24,768]{1,0:T(8,128)} async-done(((f32[768,768]{1,0:T(8,128)}), f32[24,768]{1,0:T(8,128)}) %reduce-scatter.21.cloned.1.call-update) | async-done | bytes 73744
  738.7 104.7 %reduce-scatter.23.cloned.1.call-done = f32[24,768]{1,0:T(8,128)} async-done(((f32[768,768]{1,0:T(8,128)}), f32[24,768]{1,0:T(8,128)}) %reduce-scatter.23.cloned.1.call-update) | async-done | bytes 73744
  843.4 141.0 %reduce-scatter.15.cloned.1.call-done = f32[24,3072]{1,0:T(8,128)} async-done(((f32[768,3072]{1,0:T(8,128)}), f32[24,3072]{1,0:T(8,128)}) %reduce-scatter.15.cloned.1.call-update) | async-done | bytes 294928 | tf_op jit(solution)/shard_map/reduce_scatter | solution.py:235
  984.4 141.9 %reduce-scatter.17.cloned.1.call-done = f32[96,768]{1,0:T(8,128)} async-done(((f32[3072,768]{1,0:T(8,128)}), f32[96,768]{1,0:T(8,128)}) %reduce-scatter.17.cloned.1.call-update) | async-done | bytes 294928 | tf_op jit(solution)/shard_map/reduce_scatter | solution.py:236
  (312 shorter events, 142.3 us)
Async XLA Ops:
  7.2 61.6 %copy-start.17 = (bf16[1024,768]{1,0:T(8,128)(2,1)S(1)}, bf16[1024,768]{1,0:T(8,128)(2,1)}, u32[]{:S(2)}) copy-start(bf16[1024,768]{1,0:T(8,128)(2,1)} %param.42) | copy-start | bytes 4718596
  7.2 63.8 %all-gather.7.cloned.1.call-start = ((), (), s32[]{:S(2)}) async-start(), calls=%async_computation.6 | async-start | bytes 1216512 | tf_op jit(solution)/shard_map/all_gather | solution.py:146
  7.9 115.8 %all-gather.9.cloned.1.call-start = ((), (), s32[]{:S(2)}) async-start(), calls=%async_computation.7 | async-start | bytes 1216512 | tf_op jit(solution)/shard_map/all_gather | solution.py:144
  8.7 170.9 %all-gather.11.cloned.1.call-start = ((), (), s32[]{:S(2)}) async-start(), calls=%async_computation.8 | async-start | bytes 1216512 | tf_op jit(solution)/shard_map/all_gather | solution.py:145
  9.4 226.0 %all-gather.13.cloned.1.call-start = ((), (), s32[]{:S(2)}) async-start(), calls=%async_computation.9 | async-start | bytes 1216512 | tf_op jit(solution)/shard_map/all_gather | solution.py:147
  10.0 290.7 %all-gather.15.cloned.1.call-start = ((), (), s32[]{:S(2)}) async-start(), calls=%async_computation.10 | async-start | bytes 4866048 | tf_op jit(solution)/shard_map/all_gather | solution.py:155
  10.6 355.4 %all-gather.17.cloned.1.call-start = ((), (), s32[]{:S(2)}) async-start(), calls=%async_computation.11 | async-start | bytes 4866048 | tf_op jit(solution)/shard_map/all_gather | solution.py:156
  11.2 585.9 %reduce-scatter.13.cloned.1.call-start = ((), (), s32[]{:S(2)}) async-start(), calls=%async_computation.12 | async-start | bytes 2433024 | tf_op jit(solution)/shard_map/reduce_scatter | solution.py:301
  12.0 56.6 %copy-start.59 = (s32[16]{0:T(128)}, s32[16]{0:T(128)S(1)}, u32[]{:S(2)}) copy-start(s32[16]{0:T(128)S(1)} %get-tuple-element.355) | copy-start | bytes 196
  63.9 7.1 copy-start.18
  66.6 352.8 %copy-start.45 = (f32[768]{0:T(1024)}, f32[768]{0:T(1024)S(1)}, u32[]{:S(2)}) copy-start(f32[768]{0:T(1024)S(1)} %convert_element_type.130) | copy-start | bytes 9220
  66.6 299.3 %copy-start.54 = (f32[768]{0:T(1024)}, f32[768]{0:T(1024)S(1)}, u32[]{:S(2)}) copy-start(f32[768]{0:T(1024)S(1)} %convert_element_type.131) | copy-start | bytes 9220
  68.6 6.2 copy-start.36
  77.7 46.0 %copy-start.19 = (bf16[1024,768]{1,0:T(8,128)(2,1)S(1)}, bf16[1024,768]{1,0:T(8,128)(2,1)}, u32[]{:S(2)}) copy-start(bf16[1024,768]{1,0:T(8,128)(2,1)} %param.24) | copy-start | bytes 4718596
  212.1 5.8 copy-start
  212.1 5.8 copy-start.2
  212.1 5.8 copy-start.28
  212.1 5.8 copy-start.31
  212.1 5.8 copy-start.33
  239.2 180.3 %copy-start.10 = (f32[1024,768]{0,1:T(8,128)}, f32[1024,768]{0,1:T(8,128)S(1)}, u32[]{:S(2)}) copy-start(f32[1024,768]{0,1:T(8,128)S(1)} %get-tuple-element.381) | copy-start | bytes 9437188
  239.2 180.2 %copy-start.38 = (f32[1024]{0:T(1024)}, f32[1024]{0:T(1024)S(1)}, u32[]{:S(2)}) copy-start(f32[1024]{0:T(1024)S(1)} %broadcast_multiply_fusion.1) | copy-start | bytes 12292
  239.6 179.9 %copy-start.47 = (f32[1024]{0:T(1024)}, f32[1024]{0:T(1024)S(1)}, u32[]{:S(2)}) copy-start(f32[1024]{0:T(1024)S(1)} %fusion.95) | copy-start | bytes 12292
  239.6 126.3 %copy-start.56 = (f32[768]{0:T(1024)S(1)}, f32[768]{0:T(1024)}, u32[]{:S(2)}) copy-start(f32[768]{0:T(1024)} %convert_element_type.136) | copy-start | bytes 9220
  375.4 5.5 copy-start.11
  432.0 202.9 %reduce-scatter.19.cloned.1.call-start = ((), (), s32[]{:S(2)}) async-start(), calls=%async_computation.15 | async-start | bytes 2433024
  445.6 7.2 copy-start.14
  469.9 7.1 copy-start.14
  495.8 243.0 %reduce-scatter.21.cloned.1.call-start = ((), (), s32[]{:S(2)}) async-start(), calls=%async_computation.16 | async-start | bytes 2433024
  505.2 338.2 %reduce-scatter.23.cloned.1.call-start = ((), (), s32[]{:S(2)}) async-start(), calls=%async_computation.17 | async-start | bytes 2433024
  514.5 469.9 %reduce-scatter.15.cloned.1.call-start = ((), (), s32[]{:S(2)}) async-start(), calls=%async_computation.13 | async-start | bytes 9732096 | tf_op jit(solution)/shard_map/reduce_scatter | solution.py:235
  525.2 601.2 %reduce-scatter.17.cloned.1.call-start = ((), (), s32[]{:S(2)}) async-start(), calls=%async_computation.14 | async-start | bytes 9732096 | tf_op jit(solution)/shard_map/reduce_scatter | solution.py:236
  536.9 47.6 %copy-start.23 = (bf16[96,8,2,512]{3,1,2,0:T(8,128)(2,1)S(1)}, bf16[96,8,2,512]{3,1,2,0:T(8,128)(2,1)}, u32[]{:S(2)}) copy-start(bf16[96,8,2,512]{3,1,2,0:T(8,128)(2,1)} %copy-done.22) | copy-start | bytes 4718596
  (48 other events, 110.1 us)
Sparse Core Ops, SparseCore 0:
  10.9 56.9 all-gather.6
  70.8 52.8 all-gather.8
  126.6 52.9 all-gather.10
  182.4 52.9 all-gather.12
  238.1 62.5 all-gather.14
  303.5 62.4 all-gather.16
  432.1 97.7 reduce-scatter.12
  536.6 98.1 reduce-scatter.18
  640.7 97.9 reduce-scatter.20
  745.3 98.0 reduce-scatter.22
  849.9 134.5 reduce-scatter.14
  991.8 134.5 reduce-scatter.16
where the time goes:
time: 1140 us; the launch traced here: 1130 us
  waiting for transfers between devices  735 us (64%)
  matrix products  188 us (16%)
  blocking collectives  83.2 us (7%)
  local copies, waits for them, and re-layouts  76.3 us (7%)
  other arithmetic  35 us (3%)
  between operations  15.3 us (1%)
    unnamed x15, waiting for transfers between devices  250 us
    reduce_scatter x1, waiting for transfers between devices, body(): lax.psum_scatter(grad_down, ('dp', 'fsdp'), scatter_dimension=0, tiled=True)  142 us
    reduce_scatter x1, waiting for transfers between devices, body(): lax.psum_scatter(grad_up, ('dp', 'fsdp'), scatter_dimension=0, tiled=True)  141 us
    unnamed x2, blocking collectives  83.2 us
    dot_general x6, matrix products, dense(): return jnp.dot(left, right, preferred_element_type=jnp.float32)  61.7 us
    all_gather x1, waiting for transfers between devices, body(): lax.all_gather(up_weight, ('dp', 'fsdp'), axis=0, tiled=True)  61.1 us
    all_gather x1, waiting for transfers between devices, body(): lax.all_gather(key_weight, ('dp', 'fsdp'), axis=0, tiled=True)  50.9 us
    all_gather x1, waiting for transfers between devices, body(): lax.all_gather(query_weight, ('dp', 'fsdp'), axis=0, tiled=True)  44.5 us
  transfers between devices with their start and end apart: 12, of which 10 were waited for; matrix products, arithmetic and copies ran while one was open for 20% of the time, Pallas kernels for 0%

commit v1 on v0

--- a/solution.py
+++ b/solution.py
@@ -1,9 +1,494 @@
+import functools
+import math
+
 import jax
 import jax.numpy as jnp
 from jax import lax
+from jax.experimental import pallas as pl
+from jax.experimental.pallas import tpu as pltpu
 from jax.sharding import PartitionSpec as P
 
+MESH = pl.DeviceIdType.MESH
 D = 768
+F32 = jnp.float32
+BF16 = jnp.bfloat16
+
+
+class Grid:
+    def __init__(self, nz, nf):
+        self.nz = nz
+        self.side = math.isqrt(nf // 2)
+        assert 2 * self.side * self.side == nf
+        self.chips = nz * self.side * self.side
+        self.rows = D // self.chips
+        self.dev_rows = self.rows // 2
+        self.pad = -(-self.rows // 16) * 16
+
+    def place(self):
+        s = self.side
+        self.z = lax.axis_index("dp")
+        f = lax.axis_index("fsdp")
+        self.core = lax.rem(f, 2)
+        self.lo = lax.rem(f // 2, s)
+        self.hi = f // (2 * s)
+
+    def dev(self, z, hi, lo, core):
+        return (z, (hi * self.side + lo) * 2 + core)
+
+    def sib(self):
+        return self.dev(self.z, self.hi, self.lo, 1 - self.core)
+
+    def zs(self, d):
+        return lax.rem(self.z + d, self.nz)
+
+    def los(self, d):
+        return lax.rem(self.lo + d, self.side)
+
+    def his(self, d):
+        return lax.rem(self.hi + d, self.side)
+
+    def z_peer(self, d):
+        return self.dev(self.zs(d), self.hi, self.lo, self.core)
+
+    def lo_peer(self, d):
+        return self.dev(self.z, self.hi, self.los(d), self.core)
+
+    def hi_peer(self, d):
+        return self.dev(self.z, self.his(d), self.lo, self.core)
+
+    def chip(self, z, hi, lo):
+        return (z * self.side + hi) * self.side + lo
+
+    def peers(self):
+        out = [self.sib()]
+        out += [self.z_peer(d) for d in range(1, self.nz)]
+        out += [self.lo_peer(d) for d in range(1, self.side)]
+        out += [self.hi_peer(d) for d in range(1, self.side)]
+        return out
+
+    def barrier(self):
+        sem = pltpu.get_barrier_semaphore()
+        peers = self.peers()
+        for peer in peers:
+            pl.semaphore_signal(sem, inc=1, device_id=peer, device_id_type=MESH)
+        pl.semaphore_wait(sem, len(peers))
+
+
+class Sender:
+    def __init__(self, sems):
+        self.sems = sems
+        self.started = []
+
+    def start(self, src, dst, recv_sem, device):
+        copy = pltpu.make_async_remote_copy(
+            src_ref=src,
+            dst_ref=dst,
+            send_sem=self.sems.at[len(self.started)],
+            recv_sem=recv_sem,
+            device_id=device,
+            device_id_type=MESH,
+        )
+        copy.start()
+        self.started.append(copy)
+        return copy
+
+    def arrived(self, dst, recv_sem, grid):
+        pltpu.make_async_remote_copy(
+            src_ref=dst,
+            dst_ref=dst,
+            send_sem=self.sems.at[0],
+            recv_sem=recv_sem,
+            device_id=grid.sib(),
+            device_id_type=MESH,
+        ).wait_recv()
+
+    def finish(self):
+        for copy in self.started:
+            copy.wait_send()
+
+
+class Gather:
+    def __init__(self, grid, sender, at, sem, per_core=2):
+        self.grid, self.sender, self.at, self.sem = grid, sender, at, sem
+        self.per_core = per_core
+
+    def mine(self, jj):
+        return self.grid.core * self.per_core + jj
+
+    def send(self, j, p, device):
+        self.sender.start(self.at(j, p), self.at(j, p), self.sem(j, p), device)
+
+    def wait(self, j, p):
+        self.sender.arrived(self.at(j, p), self.sem(j, p), self.grid)
+
+    def own(self):
+        g = self.grid
+        for jj in range(self.per_core):
+            j, p = self.mine(jj), g.chip(g.z, g.hi, g.lo)
+            for d in range(1, g.nz):
+                self.send(j, p, g.z_peer(d))
+            self.spread(j, p)
+
+    def spread(self, j, p):
+        g = self.grid
+        for d in range(1, g.side):
+            self.send(j, p, g.lo_peer(d))
+        for d in range(1, g.side):
+            self.send(j, p, g.hi_peer(d))
+        self.send(j, p, g.sib())
+
+    def along_z(self, d):
+        g = self.grid
+        for jj in range(self.per_core):
+            j, p = self.mine(jj), g.chip(g.zs(d), g.hi, g.lo)
+            self.wait(j, p)
+            self.spread(j, p)
+
+    def second(self, d):
+        g = self.grid
+        for jj in range(self.per_core):
+            j = self.mine(jj)
+            for e in range(1, g.side):
+                if jj % 2 == 0:
+                    p = g.chip(g.zs(d), g.hi, g.los(e))
+                else:
+                    p = g.chip(g.zs(d), g.his(e), g.lo)
+                self.wait(j, p)
+                for k in range(1, g.side):
+                    self.send(j, p, g.hi_peer(k) if jj % 2 == 0 else g.lo_peer(k))
+                self.send(j, p, g.sib())
+
+    def third(self, d):
+        g = self.grid
+        for jj in range(self.per_core):
+            j = self.mine(jj)
+            for e in range(1, g.side):
+                for k in range(g.side):
+                    if jj % 2 == 0:
+                        p = g.chip(g.zs(d), g.his(e), g.los(k))
+                    else:
+                        p = g.chip(g.zs(d), g.his(k), g.los(e))
+                    self.wait(j, p)
+                    self.send(j, p, g.sib())
+
+    def sibling(self):
+        g = self.grid
+        for jj in range(self.per_core):
+            j = (1 - g.core) * self.per_core + jj
+            for d in range(g.nz):
+                for e in range(g.side):
+                    for k in range(g.side):
+                        self.wait(j, g.chip(g.zs(d), g.his(e), g.los(k)))
+
+    @staticmethod
+    def sends(grid, per_core):
+        n, s = grid.nz, grid.side
+        return per_core * (n - 1 + n * (s - 1) + n * s * (s - 1) + grid.chips)
+
+
+def join_rows(grid, low, high):
+    parts = [low.astype(F32), high.astype(F32)]
+    if grid.pad != grid.rows:
+        parts.append(jnp.zeros((grid.pad - grid.rows, low.shape[1]), F32))
+    return jnp.concatenate(parts, axis=0).astype(BF16)
+
+
+def gather_kernel(grid, attn_ref, up_ref, down_ref, vec_ref, w_attn, w_up, w_down, w_vec,
+                  pre_ref, pre_vec, stage, stage_vec, rsem, vsem, ssem, psem, lsem):
+    grid.place()
+    grid.barrier()
+    sender = Sender(ssem)
+    c = grid.core
+    me = grid.chip(grid.z, grid.hi, grid.lo)
+    raws = (attn_ref, up_ref)
+    for g, raw in enumerate(raws):
+        for jj in range(2):
+            sender.start(raw.at[(1 - c) * 2 + jj], pre_ref.at[g, jj], psem.at[g, jj], grid.sib())
+    sender.start(vec_ref.at[1 - c], pre_vec, psem.at[2, 0], grid.sib())
+
+    groups = [
+        Gather(grid, sender, lambda j, p: w_attn.at[j, p], lambda j, p: rsem.at[0, j, p]),
+        Gather(grid, sender, lambda j, p: w_up.at[j, p], lambda j, p: rsem.at[1, j, p]),
+        Gather(grid, sender, lambda j, p: w_down.at[p, j], lambda j, p: rsem.at[2, j, p]),
+    ]
+    vec = Gather(grid, sender, lambda j, p: w_vec.at[j, p], lambda j, p: vsem.at[j, p], per_core=1)
+
+    def put(src, dst, k):
+        copy = pltpu.make_async_copy(src, dst, lsem.at[k])
+        copy.start()
+        copy.wait()
+
+    def assemble(g):
+        for jj in range(2):
+            if g < 2:
+                sender.arrived(pre_ref.at[g, jj], psem.at[g, jj], grid)
+                own, other = raws[g][c * 2 + jj], pre_ref[g, jj]
+                first = jnp.where(c == 0, own.astype(F32), other.astype(F32))
+                last = jnp.where(c == 0, other.astype(F32), own.astype(F32))
+            else:
+                first, last = down_ref[2 * jj], down_ref[2 * jj + 1]
+            stage[jj] = join_rows(grid, first, last)
+            put(stage.at[jj], groups[g].at(c * 2 + jj, me), 0)
+
+    assemble(0)
+    groups[0].own()
+    sender.arrived(pre_vec, psem.at[2, 0], grid)
+    stage_vec[...] = (vec_ref[c].astype(F32) + pre_vec[...].astype(F32)).astype(BF16)
+    put(stage_vec, w_vec.at[c, me], 0)
+    vec.own()
+    def z_steps(g):
+        for d in range(grid.nz - 1, 0, -1):
+            g.along_z(d)
+
+    def second_steps(g):
+        for d in range(grid.nz, 0, -1):
+            g.second(d)
+
+    def third_steps(g):
+        for d in range(grid.nz, 0, -1):
+            g.third(d)
+
+    z_steps(vec)
+    z_steps(groups[0])
+    assemble(1)
+    groups[1].own()
+    second_steps(vec)
+    second_steps(groups[0])
+    z_steps(groups[1])
+    assemble(2)
+    groups[2].own()
+    third_steps(vec)
+    third_steps(groups[0])
+    second_steps(groups[1])
+    z_steps(groups[2])
+    third_steps(groups[1])
+    second_steps(groups[2])
+    third_steps(groups[2])
+    for g in [vec] + groups:
+        g.sibling()
+    sender.finish()
+
+
+def gather_all(grid, raw_attn, raw_up, raw_down, raw_vec):
+    n, pad, dr = grid.chips, grid.pad, grid.dev_rows
+    nsend = 5 + 3 * Gather.sends(grid, 2) + Gather.sends(grid, 1)
+    any_spec = pl.BlockSpec(memory_space=pl.ANY)
+    vmem = pl.BlockSpec(memory_space=pltpu.VMEM)
+    return pl.pallas_call(
+        functools.partial(gather_kernel, grid),
+        out_shape=[
+            jax.ShapeDtypeStruct((4, n, pad, D), BF16),
+            jax.ShapeDtypeStruct((4, n, pad, D), BF16),
+            jax.ShapeDtypeStruct((n, 4, pad, D), BF16),
+            jax.ShapeDtypeStruct((2, n, 16, D), BF16),
+        ],
+        in_specs=[vmem] * 4,
+        out_specs=[any_spec] * 4,
+        scratch_shapes=[
+            pltpu.VMEM((2, 2, dr, D), BF16),
+            pltpu.VMEM((16, D), BF16),
+            pltpu.VMEM((2, pad, D), BF16),
+            pltpu.VMEM((16, D), BF16),
+            pltpu.SemaphoreType.DMA((3, 4, n)),
+            pltpu.SemaphoreType.DMA((2, n)),
+            pltpu.SemaphoreType.DMA((nsend,)),
+            pltpu.SemaphoreType.DMA((3, 2)),
+            pltpu.SemaphoreType.DMA((1,)),
+        ],
+        compiler_params=pltpu.CompilerParams(collective_id=0, has_side_effects=True, vmem_limit_bytes=32 * 2**20),
+    )(raw_attn, raw_up, raw_down, raw_vec)
+
+
+class Reduce:
+    def __init__(self, grid, sender, part, held, second, third, last, sems):
+        self.grid, self.sender, self.part = grid, sender, part
+        self.held, self.from_second, self.from_third, self.from_z = held, second, third, last
+        self.sem_sib, self.sem_second, self.sem_third, self.sem_z = sems
+
+    def to_sibling(self, d):
+        g = self.grid
+        z = g.zs(d)
+        for jj in range(2):
+            j = (1 - g.core) * 2 + jj
+            self.sender.start(self.part(j, z), self.held.at[jj, z], self.sem_sib.at[jj, z], g.sib())
+
+    def add_sibling(self, d):
+        g, s = self.grid, self.grid.side
+        z = g.zs(d)
+        for jj in range(2):
+            held = self.held.at[jj, z]
+            self.sender.arrived(held, self.sem_sib.at[jj, z], g)
+            own = self.part(g.core * 2 + jj, z)
+            for h in range(s):
+                def add(l, carry, h=h):
+                    held[h, l] = (held[h, l].astype(F32) + own[h, l].astype(F32)).astype(BF16)
+                    return carry
+                lax.fori_loop(0, s, add, 0)
+            for k in range(1, s):
+                if jj % 2 == 0:
+                    src, peer = held.at[g.his(k)], g.hi_peer(k)
+                else:
+                    src, peer = held.at[:, g.los(k)], g.lo_peer(k)
+                self.sender.start(src, self.from_second.at[jj, s - k - 1, z], self.sem_second.at[jj, s - k - 1, z], peer)
+
+    def add_second(self, d):
+        g, s = self.grid, self.grid.side
+        z = g.zs(d)
+        for jj in range(2):
+            for k in range(s - 1):
+                self.sender.arrived(self.from_second.at[jj, k, z], self.sem_second.at[jj, k, z], g)
+            for e in range(s):
+                at = self.held.at[jj, z, g.hi, e] if jj % 2 == 0 else self.held.at[jj, z, e, g.lo]
+                total = at[...].astype(F32)
+                for k in range(s - 1):
+                    total = total + self.from_second[jj, k, z, e].astype(F32)
+                at[...] = total.astype(BF16)
+            for k in range(1, s):
+                if jj % 2 == 0:
+                    src, peer = self.held.at[jj, z, g.hi, g.los(k)], g.lo_peer(k)
+                else:
+                    src, peer = self.held.at[jj, z, g.his(k), g.lo], g.hi_peer(k)
+                self.sender.start(src, self.from_third.at[jj, s - k - 1, z], self.sem_third.at[jj, s - k - 1, z], peer)
+
+    def own(self, jj, z):
+        g, s = self.grid, self.grid.side
+        for k in range(s - 1):
+            self.sender.arrived(self.from_third.at[jj, k, z], self.sem_third.at[jj, k, z], g)
+        total = self.held[jj, z, g.hi, g.lo].astype(F32)
+        for k in range(s - 1):
+            total = total + self.from_third[jj, k, z].astype(F32)
+        return total
+
+    def add_third(self, d):
+        g = self.grid
+        z = g.zs(d)
+        for jj in range(2):
+            at = self.held.at[jj, z, g.hi, g.lo]
+            at[...] = self.own(jj, z).astype(BF16)
+            self.sender.start(at, self.from_z.at[jj, g.nz - d - 1], self.sem_z.at[jj, g.nz - d - 1], g.z_peer(d))
+
+    def result(self, jj):
+        g = self.grid
+        total = self.own(jj, g.z)
+        for k in range(g.nz - 1):
+            self.sender.arrived(self.from_z.at[jj, k], self.sem_z.at[jj, k], g)
+            total = total + self.from_z[jj, k].astype(F32)
+        return total
+
+    @staticmethod
+    def sends(grid):
+        n, s = grid.nz, grid.side
+        return 2 * (n + n * (s - 1) * 2 + n - 1)
+
+    @staticmethod
+    def scratch(grid, groups):
+        n, s, pad = grid.nz, grid.side, grid.pad
+        return [
+            pltpu.VMEM((groups, 2, n, s, s, pad, D), BF16),
+            pltpu.VMEM((groups, 2, s - 1, n, s, pad, D), BF16),
+            pltpu.VMEM((groups, 2, s - 1, n, pad, D), BF16),
+            pltpu.VMEM((groups, 2, n - 1, pad, D), BF16),
+            pltpu.SemaphoreType.DMA((groups, 2, n)),
+            pltpu.SemaphoreType.DMA((groups, 2, s - 1, n)),
+            pltpu.SemaphoreType.DMA((groups, 2, s - 1, n)),
+            pltpu.SemaphoreType.DMA((groups, 2, n - 1)),
+        ]
+
+
+def sum_everywhere(grid, sender, own, landing, sem):
+    steps = [[grid.sib()],
+             [grid.lo_peer(d) for d in range(1, grid.side)],
+             [grid.hi_peer(d) for d in range(1, grid.side)],
+             [grid.z_peer(d) for d in range(1, grid.nz)]]
+    slot = 0
+    for n, peers in enumerate(steps):
+        for k, peer in enumerate(peers):
+            sender.start(own.at[n], landing.at[slot + len(peers) - 1 - k], sem.at[slot + len(peers) - 1 - k], peer)
+        total = own[n]
+        for k in range(len(peers)):
+            sender.arrived(landing.at[slot + k], sem.at[slot + k], grid)
+            total = total + landing[slot + k]
+        slot += len(peers)
+        own[n + 1] = total
+
+
+def peer_count(grid):
+    return 1 + 2 * (grid.side - 1) + grid.nz - 1
+
+
+def reduce_kernel(grid, g_attn, g_up, g_down, g_vec, o_attn, o_up, o_down, o_vec,
+                  held, second, third, last, s1, s2, s3, s4, swap_out, swap_in, wsem, vec, vec_in, vsem, ssem):
+    grid.place()
+    grid.barrier()
+    sender = Sender(ssem)
+    c = grid.core
+    parts = [lambda j, z: g_attn.at[j, z], lambda j, z: g_up.at[j, z], lambda j, z: g_down.at[z, :, :, j]]
+    groups = [
+        Reduce(grid, sender, parts[g], held.at[g], second.at[g], third.at[g], last.at[g],
+               (s1.at[g], s2.at[g], s3.at[g], s4.at[g]))
+        for g in range(3)
+    ]
+    order = [groups[2], groups[1], groups[0]]
+    n = grid.nz
+    for g in order:
+        for d in range(n, 0, -1):
+            g.to_sibling(d)
+    vec[0] = g_vec[...]
+    for g in order:
+        for d in range(n, 0, -1):
+            g.add_sibling(d)
+    for g in order:
+        for d in range(n, 0, -1):
+            g.add_second(d)
+    for g in order:
+        for d in range(n - 1, 0, -1):
+            g.add_third(d)
+    sum_everywhere(grid, sender, vec, vec_in, vsem)
+    o_vec[...] = vec[4]
+    r, dr = grid.rows, grid.dev_rows
+    for i, (g, out) in enumerate(((groups[1], o_up), (groups[0], o_attn))):
+        for jj in range(2):
+            total = g.result(jj)
+            top, bottom = total[:dr], total[dr:r]
+            out[c * 2 + jj] = jnp.where(c == 0, top, bottom)
+            swap_out[i, jj] = jnp.where(c == 0, bottom, top)
+            sender.start(swap_out.at[i, jj], swap_in.at[i, jj], wsem.at[i, jj], grid.sib())
+    for jj in range(2):
+        o_down[jj] = groups[2].result(jj)[:r]
+    for i, out in enumerate((o_up, o_attn)):
+        for jj in range(2):
+            sender.arrived(swap_in.at[i, jj], wsem.at[i, jj], grid)
+            out[(1 - c) * 2 + jj] = swap_in[i, jj]
+    sender.finish()
+
+
+def reduce_all(grid, g_attn, g_up, g_down, g_vec):
+    n, s, pad, dr = grid.nz, grid.side, grid.pad, grid.dev_rows
+    nsend = 3 * Reduce.sends(grid) + 4 + peer_count(grid)
+    vmem = pl.BlockSpec(memory_space=pltpu.VMEM)
+    return pl.pallas_call(
+        functools.partial(reduce_kernel, grid),
+        out_shape=[
+            jax.ShapeDtypeStruct((4, dr, D), F32),
+            jax.ShapeDtypeStruct((4, dr, D), F32),
+            jax.ShapeDtypeStruct((2, grid.rows, D), F32),
+            jax.ShapeDtypeStruct((16, D), F32),
+        ],
+        in_specs=[vmem] * 4,
+        out_specs=[vmem] * 4,
+        scratch_shapes=Reduce.scratch(grid, 3) + [
+            pltpu.VMEM((2, 2, dr, D), F32),
+            pltpu.VMEM((2, 2, dr, D), F32),
+            pltpu.SemaphoreType.DMA((2, 2)),
+            pltpu.VMEM((5, 16, D), F32),
+            pltpu.VMEM((peer_count(grid), 16, D), F32),
+            pltpu.SemaphoreType.DMA((peer_count(grid),)),
+            pltpu.SemaphoreType.DMA((nsend,)),
+        ],
+        compiler_params=pltpu.CompilerParams(collective_id=1, has_side_effects=True, vmem_limit_bytes=56 * 2**20),
+    )(g_attn, g_up, g_down, g_vec)
+
+
 HEADS = 12
 HD = 64
 ROW = 512
@@ -119,6 +604,7 @@
 
 
 def body(
+    grid,
     tokens,
     block_bucket,
     lengths,
@@ -140,41 +626,25 @@
     out_grad,
     pool_grad,
 ):
-    attn_full = (
-        lax.all_gather(query_weight, ("dp", "fsdp"), axis=0, tiled=True),
-        lax.all_gather(key_weight, ("dp", "fsdp"), axis=0, tiled=True),
-        lax.all_gather(value_weight, ("dp", "fsdp"), axis=0, tiled=True),
-        lax.all_gather(out_weight, ("dp", "fsdp"), axis=0, tiled=True),
-        lax.all_gather(query_bias, ("dp", "fsdp"), axis=0, tiled=True),
-        lax.all_gather(value_bias, ("dp", "fsdp"), axis=0, tiled=True),
-        lax.all_gather(out_bias, ("dp", "fsdp"), axis=0, tiled=True),
-        lax.all_gather(first_gain, ("dp", "fsdp"), axis=0, tiled=True),
-        lax.all_gather(first_shift, ("dp", "fsdp"), axis=0, tiled=True),
-    )
-    ffn_full = (
-        lax.all_gather(up_weight, ("dp", "fsdp"), axis=0, tiled=True),
-        lax.all_gather(down_weight, ("dp", "fsdp"), axis=0, tiled=True),
-        lax.all_gather(up_bias, ("dp", "fsdp"), axis=0, tiled=True),
-        lax.all_gather(down_bias, ("dp", "fsdp"), axis=0, tiled=True),
-        lax.all_gather(second_gain, ("dp", "fsdp"), axis=0, tiled=True),
-        lax.all_gather(second_shift, ("dp", "fsdp"), axis=0, tiled=True),
-    )
-    full_query, full_key, full_value, full_out = (
-        attn_full[0],
-        attn_full[1],
-        attn_full[2],
-        attn_full[3],
-    )
-    bias_query = attn_full[4].astype(jnp.float32)
-    bias_value = attn_full[5].astype(jnp.float32)
-    bias_out = attn_full[6].astype(jnp.float32)
-    gain_first = attn_full[7].astype(jnp.float32)
-    shift_first = attn_full[8].astype(jnp.float32)
-    full_up, full_down = (ffn_full[0], ffn_full[1])
-    bias_up = ffn_full[2].astype(jnp.float32)
-    bias_down = ffn_full[3].astype(jnp.float32)
-    gain_second = ffn_full[4].astype(jnp.float32)
-    shift_second = ffn_full[5].astype(jnp.float32)
+    rank = lax.axis_index("dp") * lax.axis_size("fsdp") + lax.axis_index("fsdp")
+    dr = grid.dev_rows
+    raw_attn = jnp.stack([query_weight, key_weight, value_weight, out_weight])
+    raw_up = up_weight.reshape(dr, 4, D).transpose(1, 0, 2)
+    raw_down = down_weight.reshape(4, dr, D)
+    small = jnp.stack([query_bias, value_bias, out_bias, first_gain, first_shift, down_bias, second_gain, second_shift])
+    small = lax.dynamic_update_slice(jnp.zeros((16, D), BF16), small, (0, rank * dr))
+    wide = lax.dynamic_update_slice(jnp.zeros((16 * D,), BF16), up_bias, (rank * 4 * dr,)).reshape(16, D)
+    w_attn, w_up, w_down, w_vec = gather_all(grid, raw_attn, raw_up, raw_down, jnp.stack([small, wide]))
+    r = grid.rows
+    w_attn = w_attn[:, :, :r].reshape(4, D, D)
+    full_query, full_key, full_value, full_out = w_attn[0], w_attn[1], w_attn[2], w_attn[3]
+    full_up = w_up[:, :, :r].reshape(4, D, D).transpose(1, 0, 2).reshape(D, 4 * D)
+    full_down = w_down[:, :, :r].reshape(4 * D, D)
+    vec = jnp.sum(w_vec.astype(F32), axis=1)
+    bias_query, bias_value, bias_out, gain_first, shift_first, bias_down, gain_second, shift_second = [vec[0, i] for i in range(8)]
+    bias_up = vec[1, :4].reshape(4 * D)
+    up_back, down_back = full_up, full_down
+    query_back, key_back, value_back, out_back = full_query, full_key, full_value, full_out
     token_start, valid, pool_matrix = sentence_layout(block_bucket, lengths, BLOCK)
     row_count = tokens.shape[0] // ROW
 
@@ -208,15 +678,6 @@
     pools, pool_back = jax.vjp(
         lambda rows_in: matryoshka(product(pool_matrix, rows_in), D), outputs
     )
-    ffn_back = (
-        lax.all_gather(up_weight, ("dp", "fsdp"), axis=0, tiled=True),
-        lax.all_gather(down_weight, ("dp", "fsdp"), axis=0, tiled=True),
-        lax.all_gather(up_bias, ("dp", "fsdp"), axis=0, tiled=True),
-        lax.all_gather(down_bias, ("dp", "fsdp"), axis=0, tiled=True),
-        lax.all_gather(second_gain, ("dp", "fsdp"), axis=0, tiled=True),
-        lax.all_gather(second_shift, ("dp", "fsdp"), axis=0, tiled=True),
-    )
-    up_back, down_back = (ffn_back[0], ffn_back[1])
     out_total = out_grad.astype(jnp.float32) + pool_back(pool_grad)[0]
     grad_second_sum, grad_gain_second, grad_shift_second = second_back(out_total)
     grad_branch = grad_second_sum.astype(jnp.bfloat16)
@@ -230,31 +691,6 @@
     grad_up = jnp.einsum("td,tf->df", hidden_low, grad_pre, preferred_element_type=jnp.float32)
     grad_hidden = grad_second_sum + jnp.einsum(
         "tf,df->td", grad_pre, up_back, preferred_element_type=jnp.float32
-    )
-    ffn_grads = (
-        lax.psum_scatter(grad_up, ("dp", "fsdp"), scatter_dimension=0, tiled=True),
-        lax.psum_scatter(grad_down, ("dp", "fsdp"), scatter_dimension=0, tiled=True),
-        lax.psum_scatter(grad_bias_up, ("dp", "fsdp"), scatter_dimension=0, tiled=True),
-        lax.psum_scatter(grad_bias_down, ("dp", "fsdp"), scatter_dimension=0, tiled=True),
-        lax.psum_scatter(grad_gain_second, ("dp", "fsdp"), scatter_dimension=0, tiled=True),
-        lax.psum_scatter(grad_shift_second, ("dp", "fsdp"), scatter_dimension=0, tiled=True),
-    )
-    attn_back = (
-        lax.all_gather(query_weight, ("dp", "fsdp"), axis=0, tiled=True),
-        lax.all_gather(key_weight, ("dp", "fsdp"), axis=0, tiled=True),
-        lax.all_gather(value_weight, ("dp", "fsdp"), axis=0, tiled=True),
-        lax.all_gather(out_weight, ("dp", "fsdp"), axis=0, tiled=True),
-        lax.all_gather(query_bias, ("dp", "fsdp"), axis=0, tiled=True),
-        lax.all_gather(value_bias, ("dp", "fsdp"), axis=0, tiled=True),
-        lax.all_gather(out_bias, ("dp", "fsdp"), axis=0, tiled=True),
-        lax.all_gather(first_gain, ("dp", "fsdp"), axis=0, tiled=True),
-        lax.all_gather(first_shift, ("dp", "fsdp"), axis=0, tiled=True),
-    )
-    query_back, key_back, value_back, out_back = (
-        attn_back[0],
-        attn_back[1],
-        attn_back[2],
-        attn_back[3],
     )
     grad_first_sum, grad_gain_first, grad_shift_first = first_back(grad_hidden)
     grad_attended = grad_first_sum.astype(jnp.bfloat16)
@@ -294,36 +730,39 @@
     token_grad = token_grad + jnp.einsum(
         "te,de->td", grad_values, value_back, preferred_element_type=jnp.float32
     )
-    attn_grads = (
-        lax.psum_scatter(grad_query, ("dp", "fsdp"), scatter_dimension=0, tiled=True),
-        lax.psum_scatter(grad_key, ("dp", "fsdp"), scatter_dimension=0, tiled=True),
-        lax.psum_scatter(grad_value, ("dp", "fsdp"), scatter_dimension=0, tiled=True),
-        lax.psum_scatter(grad_out, ("dp", "fsdp"), scatter_dimension=0, tiled=True),
-        lax.psum_scatter(grad_bias_query, ("dp", "fsdp"), scatter_dimension=0, tiled=True),
-        lax.psum_scatter(grad_bias_value, ("dp", "fsdp"), scatter_dimension=0, tiled=True),
-        lax.psum_scatter(grad_bias_out, ("dp", "fsdp"), scatter_dimension=0, tiled=True),
-        lax.psum_scatter(grad_gain_first, ("dp", "fsdp"), scatter_dimension=0, tiled=True),
-        lax.psum_scatter(grad_shift_first, ("dp", "fsdp"), scatter_dimension=0, tiled=True),
-    )
+    def blocks(grad):
+        low = grad.astype(BF16).reshape(-1, grid.rows, D)
+        return jnp.pad(low, ((0, 0), (0, grid.pad - grid.rows), (0, 0)))
+
+    n, s, pad = grid.nz, grid.side, grid.pad
+    g_attn = jnp.stack([blocks(grad_query), blocks(grad_key), blocks(grad_value), blocks(grad_out)]).reshape(4, n, s, s, pad, D)
+    g_up = jnp.stack([blocks(grad_up[:, j * D : (j + 1) * D]) for j in range(4)]).reshape(4, n, s, s, pad, D)
+    g_down = blocks(grad_down).reshape(n, s, s, 4, pad, D)
+    g_vec = jnp.concatenate([
+        jnp.stack([grad_bias_query, grad_bias_value, grad_bias_out, grad_gain_first, grad_shift_first, grad_bias_down, grad_gain_second, grad_shift_second]),
+        grad_bias_up.reshape(4, D), jnp.zeros((4, D), F32)])
+    o_attn, o_up, o_down, o_vec = reduce_all(grid, g_attn, g_up, g_down, g_vec)
+    small = lax.dynamic_slice(o_vec, (0, rank * dr), (8, dr))
+    wide = lax.dynamic_slice(o_vec[8:12].reshape(4 * D), (rank * 4 * dr,), (4 * dr,))
     return (
         outputs.astype(jnp.bfloat16),
         pools,
         token_grad,
-        attn_grads[0],
-        attn_grads[4],
-        attn_grads[1],
-        attn_grads[2],
-        attn_grads[5],
-        attn_grads[3],
-        attn_grads[6],
-        attn_grads[7],
-        attn_grads[8],
-        ffn_grads[0],
-        ffn_grads[2],
-        ffn_grads[1],
-        ffn_grads[3],
-        ffn_grads[4],
-        ffn_grads[5],
+        o_attn[0],
+        small[0],
+        o_attn[1],
+        o_attn[2],
+        small[1],
+        o_attn[3],
+        small[2],
+        small[3],
+        small[4],
+        o_up.transpose(1, 0, 2).reshape(dr, 4 * D),
+        wide,
+        o_down.reshape(4 * dr, D),
+        small[5],
+        small[6],
+        small[7],
     )
 
 
@@ -351,7 +790,7 @@
         P(("dp", "fsdp"), None),
     )
     return jax.shard_map(
-        body,
+        functools.partial(body, Grid(mesh.shape["dp"], mesh.shape["fsdp"])),
         mesh=mesh,
         in_specs=placed,
         out_specs=(

time: 1140 us -> 486 us (0.43)
  waiting for transfers between devices: 735 us -> 0 us
  Pallas kernels: 0 us -> 186 us
  blocking collectives: 83.2 us -> 0 us
  matrix products: 188 us -> 169 us
  between operations: 15.3 us -> 2.2 us
    reduce_scatter x3 -> x0, waiting for transfers between devices: 283 us -> none  [the longest x1 142 us: body(): lax.psum_scatter(grad_down, ('dp', 'fsdp'), scatter_dimension=0, tiled=True)]
    unnamed x15 -> x0, waiting for transfers between devices: 250 us -> none
    all_gather x6 -> x0, waiting for transfers between devices: 202 us -> none  [the longest x1 61.1 us: body(): lax.all_gather(up_weight, ('dp', 'fsdp'), axis=0, tiled=True)]
    pallas_call x0 -> x2, Pallas kernels: none -> 186 us  [the longest x1 99.8 us: reduce_all(): pl.pallas_call(functools.partial(reduce_kernel, grid), out_shape=[jax.Sha...]
    unnamed x2 -> x0, blocking collectives: 83.2 us -> none
    unnamed x154 -> x165, local copies, waits for them, and re-layouts: 43.4 us -> 28.4 us
  transfers between devices with their start and end apart: 12 -> 0, of which waited for: 10 -> 0; matrix products, arithmetic and copies ran while one was open for 20% -> 0% of each run, Pallas kernels for 0% -> 0%
where the time goes in v1:
time: 486 us; the launch traced here: 478 us
  Pallas kernels  186 us (38%)
  matrix products  169 us (35%)
  local copies, waits for them, and re-layouts  80.4 us (17%)
  other arithmetic  39 us (8%)
    pallas_call x1, Pallas kernels, reduce_all(): pl.pallas_call(functools.partial(reduce_kernel, grid), out_shape=[jax.Sha...  99.8 us
    pallas_call x1, Pallas kernels, gather_all(): pl.pallas_call(functools.partial(gather_kernel, grid), out_shape=[jax.Sha...  86.6 us
    dot_general x6, matrix products, dense(): return jnp.dot(left, right, preferred_element_type=jnp.float32)  53.9 us
    unnamed x165, local copies, waits for them, and re-layouts  28.4 us
    dot_general x1, matrix products, body(): jnp.einsum('td,fd->tf', grad_branch, down_back, preferred_element_type=jn...  16.7 us
    convert_element_type x2, other arithmetic, attend_backward(): grad_scores = (softmax_out * (grad_probs - row_delta)).astype(jnp.bfloat16)  14.2 us
    dot_general x2, matrix products, attend_backward(): jnp.einsum('qhd,khd->hqk', grad_rows, value_rows, preferred_element_type=...  13.8 us
    dot_general x1, matrix products, body(): jnp.einsum('tf,df->td', grad_pre, up_back, preferred_element_type=jnp.flo...  11.7 us

profile of v1, /device:TPU:0, one launch (start us, length us, event | category | flops | bytes accessed | tf_op | source)
XLA Modules:
  0.0 477.8 jit_solution(17316615908807379504)
XLA Ops:
  5.4 86.6 %shard_map.331 = (bf16[4,16,48,768]{3,2,1,0:T(8,128)(2,1)S(1)}, bf16[4,16,48,768]{3,2,1,0:T(8,128)(2,1)S(1)}, bf16[16,4,48,768]{3,2,1,0:T(8,128)(2,1)S(1)}, bf16[2,16,16,768]{3,2,1,0:T(8,128)(2,1)S(1)}) custom-call(bf16[4,24,768]{2,1,0:T(8,128)(2,1)S(1)} %pad_maximum_fusion.2.attn_ref, bf16[4,24,768]{2,1,0:T(8,128)(2,1)S(1)} %bitcast.249, ...), custom_call_target="tpu_custom_call" | custom-call | tf_op jit(solution)/shard_map/pallas_call | solution.py:277
  102.3 2.6 fusion.71
  104.9 2.9 reshape.458
  118.8 21.1 %while.26 = (s32[]{:T(128)}, bf16[2,512,12,64]{1,3,2,0:T(8,128)(2,1)}, f32[2,12,512,1]{2,1,3,0:T(8,128)S(1)}, bf16[2,512,12,64]{1,3,2,0:T(8,128)(2,1)}, s32[2,51...) while((s32[]{:T(128)}, ...), condition=%wide.region_5.6_spmd, body=%wide.region_2.5_spmd.sunk | while | flops 843966464 | bytes 42174056 | solution.py:660
  121.4 2.6 fusion.174
  124.0 5.5 %fusion.175 = bf16[2,512,12,64]{1,3,2,0:T(8,128)(2,1)} fusion(bf16[2,512,12,64]{1,3,2,0:T(8,128)(2,1)} %get-tuple-element.517, s32[]{:T(128)} %get-tuple-element.516, f32[12,512,512]{1,2,0:T(8,128)S(1)} %get-tuple-element.492, f32[12,512]{1,0:T(8,128)S(1)} %fusion.174, f32[12,512]{1,0:T(8,128)S(1)} %get-tuple-element.493, ...), kind=kOutput, calls=%fused_computation.8.clone.1 | convolution fusion | flops 418775040 | bytes 14468096 | tf_op jit(solution)/shard_map/while/body/eval_jaxpr/hqk,khd->qhd/dot_general | solution.py:570
  131.8 2.6 fusion.174
  134.4 5.5 %fusion.175 = bf16[2,512,12,64]{1,3,2,0:T(8,128)(2,1)} fusion(bf16[2,512,12,64]{1,3,2,0:T(8,128)(2,1)} %get-tuple-element.517, s32[]{:T(128)} %get-tuple-element.516, f32[12,512,512]{1,2,0:T(8,128)S(1)} %get-tuple-element.492, f32[12,512]{1,0:T(8,128)S(1)} %fusion.174, f32[12,512]{1,0:T(8,128)S(1)} %get-tuple-element.493, ...), kind=kOutput, calls=%fused_computation.8.clone.1 | convolution fusion | flops 418775040 | bytes 14468096 | tf_op jit(solution)/shard_map/while/body/eval_jaxpr/hqk,khd->qhd/dot_general | solution.py:570
  139.9 4.2 copy.95
  147.6 2.9 fusion.116
  153.4 6.8 %copy.96 = bf16[4,768,768]{1,2,0:T(8,128)(2,1)} copy(bf16[4,768,768]{2,1,0:T(8,128)(2,1)} %bitcast.248) | data formatting | bytes 9437184 | tf_op jit(solution)/shard_map/reshape | solution.py:641
  160.2 38.0 %multiply_convert_fusion.3 = (bf16[1024,3072]{1,0:T(8,128)(2,1)S(1)}, f32[1024,3072]{1,0:T(8,128)}, f32[1024,3072]{1,0:T(8,128)}) fusion(f32[3072]{0:T(1024)S(1)} %add.225, bf16[768,3072]{0,1:T(8,128)(2,1)} %bitcast.269, f32[1024,768]{0,1:T(8,128)} %copy-done.16, f32[768]{0:T(1024)S(1)} %copy-done.68, f32[768]{0:T(1024)S(1)} %copy-done.60, ...), kind=kOutput, calls=%fused_computation.70 | convolution fusion | flops 5043388416 | bytes 39348224 | tf_op jit(solution)/shard_map/dot_general | solution.py:499
  198.2 7.5 %fusion.117 = (f32[1024]{0:T(1024)S(1)}, f32[1024,768]{0,1:T(8,128)}) fusion(f32[768]{0:T(1024)S(1)} %copy-done.70, bf16[1024,3072]{1,0:T(8,128)(2,1)S(1)} %get-tuple-element.322, bf16[3072,768]{1,0:T(8,128)(2,1)S(1)} %bitcast.253, f32[768]{0:T(1024)S(1)} %copy-done.68, f32[768]{0:T(1024)S(1)} %copy-done.60, f32[1024]{0:T(1024)S(1)} %fusion.98, ...), kind=kOutput, calls=%fused_computation.243 | convolution fusion | flops 4838915072 | bytes 17323008 | tf_op jit(solution)/shard_map/dot_general | solution.py:499
  208.4 4.9 %multiply_reduce_fusion.7 = (f32[16]{0:T(128)S(1)}, f32[16]{0:T(128)S(1)}, f32[16,768]{1,0:T(8,128)S(1)}) fusion(f32[16,1728]{1,0:T(8,128)S(1)} %copy-done.46, f32[1024,768]{0,1:T(8,128)} %get-tuple-element.373, f32[768]{0:T(1024)S(1)} %copy-done.62, f32[768]{0:T(1024)S(1)} %copy-done.52, f32[1024]{0:T(1024)S(1)} %fusion.99, ...), kind=kOutput, calls=%fused_computation.138 | convolution fusion | flops 154255328 | bytes 3263744 | tf_op jit(solution)/shard_map/jvp()/dot_general | solution.py:503
  216.1 6.4 %multiply_reduce_fusion.1 = (f32[768]{0:T(1024)}, f32[1024]{0:T(1024)S(1)}, f32[768]{0:T(1024)}, f32[1024,768]{0,1:T(8,128)S(1)}) fusion(f32[1024,768]{0,1:T(8,128)} %get-tuple-element.373, f32[1024]{0:T(1024)S(1)} %fusion.99, f32[1024]{0:T(1024)S(1)} %broadcast_multiply_fusion, f32[768]{0:T(1024)S(1)} %copy-done.52, f32[16,768]{1,0:T(8,128)S(1)} %get-tuple-element.374, ...), kind=kOutput, calls=%fused_computation.90 | convolution fusion | flops 159020544 | bytes 8057856 | tf_op jit(solution)/shard_map/transpose(jvp())/dot_general | solution.py:503
  222.6 4.0 fusion.111
  229.2 16.7 %convert_reduce_fusion = (f32[3072]{0:T(1024)}, bf16[1024,3072]{1,0:T(8,128)(2,1)}) fusion(f32[1024,3072]{1,0:T(8,128)} %get-tuple-element.323, bf16[1024,768]{0,1:T(8,128)(2,1)S(1)} %get-tuple-element.315, bf16[3072,768]{1,0:T(8,128)(2,1)S(1)} %bitcast.256, f32[1024,3072]{1,0:T(8,128)} %get-tuple-element.371, f32[3072]{0:T(1024)S(1)} %add.225), kind=kOutput, calls=%fused_computation.68 | convolution fusion | flops 4885312512 | bytes 37773312 | tf_op jit(solution)/shard_map/td,fd->tf/dot_general | solution.py:686
  245.9 11.7 %multiply_reduce_fusion.2 = (f32[768]{0:T(1024)}, f32[1024]{0:T(1024)S(1)}, f32[768]{0:T(1024)}, f32[1024,768]{0,1:T(8,128)S(1)}) fusion(f32[1024,768]{0,1:T(8,128)} %copy-done.16, f32[1024]{0:T(1024)S(1)} %fusion.98, f32[1024]{0:T(1024)S(1)} %broadcast_multiply_fusion.1, f32[768]{0:T(1024)S(1)} %copy-done.60, bf16[1024,3072]{1,0:T(8,128)(2,1)} %get-tuple-element.378, ...), kind=kOutput, calls=%fused_computation.92 | convolution fusion | flops 4839699456 | bytes 20472832 | tf_op jit(solution)/shard_map/tf,df->td/dot_general | solution.py:692
  271.2 49.2 %while.27 = (s32[]{:T(128)}, bf16[2,512,12,64]{1,3,2,0:T(8,128)(2,1)}, bf16[2,512,12,64]{1,3,2,0:T(8,128)(2,1)}, bf16[2,512,12,64]{1,3,2,0:T(8,128)(2,1)}, bf16[...) while((s32[]{:T(128)}, ...), condition=%wide.region_26.27_spmd, body=%wide.region_24.26_spmd.sunk | while | flops 2062936064 | bytes 147526480 | solution.py:704
  273.6 6.9 %multiply_reduce_fusion.18 = (f32[12,512]{1,0:T(8,128)S(1)}, f32[12,512,512]{1,2,0:T(8,128)}) fusion(f32[12,512,512]{1,2,0:T(8,128)S(1)} %fusion.184, f32[12,512]{1,0:T(8,128)S(1)} %dynamic-slice_bitcast_fusion.2, pred[512,512]{0,1:T(8,128)(4,1)S(1)} %compare_and_fusion.5, bf16[2,512,12,64]{1,3,2,0:T(8,128)(2,1)S(1)} %copy-done.9, ...), kind=kOutput, calls=%fused_computation.25.clone.1 | convolution fusion | flops 418375680 | bytes 27059200 | tf_op jit(solution)/shard_map/while/body/eval_jaxpr/qhd,khd->hqk/dot_general | solution.py:586
  280.5 7.1 %multiply_convert_fusion.5 = bf16[12,512,512]{1,2,0:T(8,128)(2,1)S(1)} fusion(f32[12,512,512]{1,2,0:T(8,128)} %get-tuple-element.505, f32[12,512,512]{1,2,0:T(8,128)S(1)} %fusion.184, f32[12,512]{1,0:T(8,128)S(1)} %get-tuple-element.506, f32[12,512]{1,0:T(8,128)S(1)} %dynamic-slice_bitcast_fusion.2, pred[512,512]{0,1:T(8,128)(4,1)S(1)} %compare_and_fusion.5), kind=kLoop, calls=%fused_computation.24.clone.1 | loop fusion | flops 18874368 | bytes 31768576 | tf_op jit(solution)/shard_map/while/body/eval_jaxpr/convert_element_type | solution.py:590
  292.0 3.9 fusion.187
  298.1 6.9 %multiply_reduce_fusion.18 = (f32[12,512]{1,0:T(8,128)S(1)}, f32[12,512,512]{1,2,0:T(8,128)}) fusion(f32[12,512,512]{1,2,0:T(8,128)S(1)} %fusion.184, f32[12,512]{1,0:T(8,128)S(1)} %dynamic-slice_bitcast_fusion.2, pred[512,512]{0,1:T(8,128)(4,1)S(1)} %compare_and_fusion.5, bf16[2,512,12,64]{1,3,2,0:T(8,128)(2,1)S(1)} %copy-done.9, ...), kind=kOutput, calls=%fused_computation.25.clone.1 | convolution fusion | flops 418375680 | bytes 27059200 | tf_op jit(solution)/shard_map/while/body/eval_jaxpr/qhd,khd->hqk/dot_general | solution.py:586
  305.0 7.1 %multiply_convert_fusion.5 = bf16[12,512,512]{1,2,0:T(8,128)(2,1)S(1)} fusion(f32[12,512,512]{1,2,0:T(8,128)} %get-tuple-element.505, f32[12,512,512]{1,2,0:T(8,128)S(1)} %fusion.184, f32[12,512]{1,0:T(8,128)S(1)} %get-tuple-element.506, f32[12,512]{1,0:T(8,128)S(1)} %dynamic-slice_bitcast_fusion.2, pred[512,512]{0,1:T(8,128)(4,1)S(1)} %compare_and_fusion.5), kind=kLoop, calls=%fused_computation.24.clone.1 | loop fusion | flops 18874368 | bytes 31768576 | tf_op jit(solution)/shard_map/while/body/eval_jaxpr/convert_element_type | solution.py:590
  316.5 3.9 fusion.187
  320.5 2.5 convert_reduce_fusion.3
  324.6 9.8 %convolution_convert_fusion = bf16[3072,768]{1,0:T(8,128)(2,1)} fusion(bf16[1024,3072]{1,0:T(8,128)(2,1)} %copy-done.80, bf16[1024,768]{0,1:T(8,128)(2,1)S(1)} %copy-done.36), kind=kOutput, calls=%fused_computation.84 | convolution fusion | flops 4834197504 | bytes 12582912 | tf_op jit(solution)/shard_map/tf,td->fd/dot_general | solution.py:685
  334.5 5.9 %convolution_convert_fusion.1 = bf16[768,3072]{1,0:T(8,128)(2,1)S(1)} fusion(bf16[1024,3072]{1,0:T(8,128)(2,1)S(1)} %copy-done.79, f32[1024,768]{0,1:T(8,128)S(1)} %copy-done.19, f32[768]{0:T(1024)S(1)} %copy-done.69, f32[768]{0:T(1024)S(1)} %copy-done.61, f32[1024]{0:T(1024)S(1)} %copy-done.66, f32[1024]{0:T(1024)S(1)} %copy-done.54), kind=kOutput, calls=%fused_computation.85 | convolution fusion | flops 4838129664 | bytes 14170112 | tf_op jit(solution)/shard_map/td,tf->df/dot_general | solution.py:691
  354.4 4.5 pad_maximum_fusion
  358.9 99.8 %shard_map.332 = (f32[4,24,768]{2,1,0:T(8,128)}, f32[4,24,768]{2,1,0:T(8,128)}, f32[2,48,768]{2,1,0:T(8,128)}, f32[16,768]{1,0:T(8,128)}) custom-call(bf16[4,4,2,2,48,768]{5,4,3,2,1,0:T(8,128)(2,1)} %get-tuple-element.381.g_attn, bf16[4,4,2,2,48,768]{5,4,3,2,1,0:T(8,128)(2,1)} %get-tuple-element.382.g_up, bf16[4,2,2,4,48,768]{5,4,3,2,1,0:T(8,128)(2,1)} %bitcast.271, ...), custom_call_target="tpu_custom_call" | custom-call | tf_op jit(solution)/shard_map/pallas_call | solution.py:469
  464.8 2.7 fusion.118
  474.1 2.6 copy.112
  (318 shorter events, 99.9 us)
Async XLA Ops:
  92.0 4.8 copy-start.2
  93.0 4.8 %copy-start.29 = (bf16[1024,768]{1,0:T(8,128)(2,1)S(1)}, bf16[1024,768]{1,0:T(8,128)(2,1)}, u32[]{:S(2)}) copy-start(bf16[1024,768]{1,0:T(8,128)(2,1)} %param.24) | copy-start | bytes 4718596
  111.6 4.1 copy-start.77
  111.6 5.0 %copy-start.78 = (s32[16]{0:T(128)S(1)}, s32[16]{0:T(128)}, u32[]{:S(2)}) copy-start(s32[16]{0:T(128)} %param.26) | copy-start | bytes 196
  139.9 5.8 %copy-start.3 = (bf16[2,512,12,64]{1,3,2,0:T(8,128)(2,1)}, bf16[2,512,12,64]{1,3,2,0:T(8,128)(2,1)S(1)}, u32[]{:S(2)}) copy-start(bf16[2,512,12,64]{1,3,2,0:T(8,128)(2,1)S(1)} %get-tuple-element.606) | copy-start | bytes 4718596
  139.9 5.8 %copy-start.5 = (bf16[2,512,12,64]{1,3,2,0:T(8,128)(2,1)}, bf16[2,512,12,64]{1,3,2,0:T(8,128)(2,1)S(1)}, u32[]{:S(2)}) copy-start(bf16[2,512,12,64]{1,3,2,0:T(8,128)(2,1)S(1)} %get-tuple-element.607) | copy-start | bytes 4718596
  139.9 5.8 %copy-start.43 = (f32[2,12,512,1]{2,1,3,0:T(8,128)}, f32[2,12,512,1]{2,1,3,0:T(8,128)S(1)}, u32[]{:S(2)}) copy-start(f32[2,12,512,1]{2,1,3,0:T(8,128)S(1)} %get-tuple-element.542) | copy-start | bytes 147460
  139.9 5.8 %copy-start.47 = (pred[2,512]{1,0:T(4,128)(4,1)}, pred[2,512]{1,0:T(4,128)(4,1)S(1)}, u32[]{:S(2)}) copy-start(pred[2,512]{1,0:T(4,128)(4,1)S(1)} %get-tuple-element.609) | copy-start | bytes 3076
  139.9 5.8 %copy-start.49 = (s32[2,512]{1,0:T(2,128)}, s32[2,512]{1,0:T(2,128)S(1)}, u32[]{:S(2)}) copy-start(s32[2,512]{1,0:T(2,128)S(1)} %get-tuple-element.610) | copy-start | bytes 12292
  150.5 107.1 %copy-start.53 = (f32[1024]{0:T(1024)}, f32[1024]{0:T(1024)S(1)}, u32[]{:S(2)}) copy-start(f32[1024]{0:T(1024)S(1)} %broadcast_multiply_fusion.1) | copy-start | bytes 12292
  152.6 105.1 %copy-start.65 = (f32[1024]{0:T(1024)}, f32[1024]{0:T(1024)S(1)}, u32[]{:S(2)}) copy-start(f32[1024]{0:T(1024)S(1)} %fusion.98) | copy-start | bytes 12292
  153.3 6.8 %copy-start.60 = (f32[768]{0:T(1024)S(1)}, f32[768]{0:T(1024)}, u32[]{:S(2)}) copy-start(f32[768]{0:T(1024)} %get-tuple-element.262) | copy-start | bytes 9220
  153.3 6.8 %copy-start.68 = (f32[768]{0:T(1024)S(1)}, f32[768]{0:T(1024)}, u32[]{:S(2)}) copy-start(f32[768]{0:T(1024)} %get-tuple-element.261) | copy-start | bytes 9220
  153.4 44.8 %slice-start = ((s8[4718592]{0:T(1024)(128)(4,1)}), s8[524288]{0:T(1024)(128)(4,1)S(1)}, s32[]{:S(2)}) async-start(s8[4718592]{0:T(1024)(128)(4,1)} %bitcast.251), calls=%async_computation | async-start | bytes 1048576
  160.1 38.0 %slice-start.1 = ((s8[4718592]{0:T(1024)(128)(4,1)}), s8[4194304]{0:T(1024)(128)(4,1)S(1)}, s32[]{:S(2)}) async-start(s8[4718592]{0:T(1024)(128)(4,1)} %bitcast.251), calls=%async_computation.1 | async-start | bytes 8388608
  160.1 38.0 %copy-start.17 = (f32[1024,768]{0,1:T(8,128)S(1)}, f32[1024,768]{0,1:T(8,128)}, u32[]{:S(2)}) copy-start(f32[1024,768]{0,1:T(8,128)} %copy-done.16) | copy-start | bytes 9437188
  160.2 38.0 %copy-start.70 = (f32[768]{0:T(1024)S(1)}, f32[768]{0:T(1024)}, u32[]{:S(2)}) copy-start(f32[768]{0:T(1024)} %get-tuple-element.260) | copy-start | bytes 9220
  198.1 7.5 %copy-start.80 = (bf16[1024,3072]{1,0:T(8,128)(2,1)}, bf16[1024,3072]{1,0:T(8,128)(2,1)S(1)}, u32[]{:S(2)}) copy-start(bf16[1024,3072]{1,0:T(8,128)(2,1)S(1)} %get-tuple-element.322) | copy-start | bytes 18874372
  205.7 9.3 %copy-start.28 = (bf16[1024,768]{1,0:T(8,128)(2,1)S(1)}, bf16[1024,768]{1,0:T(8,128)(2,1)}, u32[]{:S(2)}) copy-start(bf16[1024,768]{1,0:T(8,128)(2,1)} %param.42) | copy-start | bytes 4718596
  222.6 6.6 %slice-start.2 = ((s8[4718592]{0:T(1024)(128)(4,1)}), s8[4194304]{0:T(1024)(128)(4,1)S(1)}, s32[]{:S(2)}) async-start(s8[4718592]{0:T(1024)(128)(4,1)} %bitcast.254), calls=%async_computation.2 | async-start | bytes 8388608
  222.6 6.6 %slice-start.3 = ((s8[4718592]{0:T(1024)(128)(4,1)}), s8[524288]{0:T(1024)(128)(4,1)S(1)}, s32[]{:S(2)}) async-start(s8[4718592]{0:T(1024)(128)(4,1)} %bitcast.254), calls=%async_computation.3 | async-start | bytes 1048576
  229.2 16.8 %copy-start.35 = (bf16[1024,768]{0,1:T(8,128)(2,1)}, bf16[1024,768]{0,1:T(8,128)(2,1)S(1)}, u32[]{:S(2)}) copy-start(bf16[1024,768]{0,1:T(8,128)(2,1)S(1)} %get-tuple-element.315) | copy-start | bytes 4718596
  245.9 11.8 %copy-start.18 = (f32[1024,768]{0,1:T(8,128)S(1)}, f32[1024,768]{0,1:T(8,128)}, u32[]{:S(2)}) copy-start(f32[1024,768]{0,1:T(8,128)} %copy-done.16) | copy-start | bytes 9437188
  280.5 7.1 %copy-start.23 = (bf16[2,512,12,64]{1,3,2,0:T(8,128)(2,1)S(1)}, bf16[2,512,12,64]{1,3,2,0:T(8,128)(2,1)}, u32[]{:S(2)}) copy-start(bf16[2,512,12,64]{1,3,2,0:T(8,128)(2,1)} %get-tuple-element.548) | copy-start | bytes 4718596 | tf_op jit(solution)/shard_map/while
  305.0 7.1 %copy-start.23 = (bf16[2,512,12,64]{1,3,2,0:T(8,128)(2,1)S(1)}, bf16[2,512,12,64]{1,3,2,0:T(8,128)(2,1)}, u32[]{:S(2)}) copy-start(bf16[2,512,12,64]{1,3,2,0:T(8,128)(2,1)} %get-tuple-element.548) | copy-start | bytes 4718596 | tf_op jit(solution)/shard_map/while
  320.5 4.1 copy-start.36
  324.6 9.9 %copy-start.19 = (f32[1024,768]{0,1:T(8,128)S(1)}, f32[1024,768]{0,1:T(8,128)}, u32[]{:S(2)}) copy-start(f32[1024,768]{0,1:T(8,128)} %copy-done.16) | copy-start | bytes 9437188
  324.6 9.9 %copy-start.54 = (f32[1024]{0:T(1024)S(1)}, f32[1024]{0:T(1024)}, u32[]{:S(2)}) copy-start(f32[1024]{0:T(1024)} %copy-done.53) | copy-start | bytes 12292
  324.6 9.9 %copy-start.61 = (f32[768]{0:T(1024)S(1)}, f32[768]{0:T(1024)}, u32[]{:S(2)}) copy-start(f32[768]{0:T(1024)} %get-tuple-element.262) | copy-start | bytes 9220
  324.6 9.9 %copy-start.66 = (f32[1024]{0:T(1024)S(1)}, f32[1024]{0:T(1024)}, u32[]{:S(2)}) copy-start(f32[1024]{0:T(1024)} %copy-done.65) | copy-start | bytes 12292
  324.6 9.9 %copy-start.69 = (f32[768]{0:T(1024)S(1)}, f32[768]{0:T(1024)}, u32[]{:S(2)}) copy-start(f32[768]{0:T(1024)} %get-tuple-element.261) | copy-start | bytes 9220
  324.6 9.9 %copy-start.79 = (bf16[1024,3072]{1,0:T(8,128)(2,1)S(1)}, bf16[1024,3072]{1,0:T(8,128)(2,1)}, u32[]{:S(2)}) copy-start(bf16[1024,3072]{1,0:T(8,128)(2,1)} %get-tuple-element.378) | copy-start | bytes 18874372
  (60 other events, 128.9 us)
